TPU v7x, 32 devices: a whole 2x2x4 slice. The times are simulated.
32 devices in a mesh: dp: 8 (over z, x), expert: 4 (over y, core).
Axes of the slice: x: 2, y: 2, z: 4, core: 2. Of those that a mesh axis runs over, the one named last changes fastest.
Arguments:
- tokens: bfloat16 [2048, 4096], P('dp', 'expert'), may hold values from -6 to 6
- route_ids: int32 [2048, 8], P('dp'), may hold values from 0 to 31, all different within a row; in each aligned block of 256 rows (0 to 255, 256 to 511, ...) at most 128 rows name the same one
- route_gates: float32 [2048, 8], P('dp'), may hold values from 0.05 to 1
- gate_weight: bfloat16 [4, 6144, 4096], P('expert', 'dp'), may hold values from -0.09375 to 0.09375
- up_weight: bfloat16 [4, 6144, 4096], P('expert', 'dp'), may hold values from -0.09375 to 0.09375
- down_weight: bfloat16 [4, 6144, 4096], P('expert', 'dp'), may hold values from -0.21875 to 0.21875
Outputs:
- mixed: bfloat16 [2048, 4096], P('dp', 'expert')
Inputs may be any that keep to these rules, and one draw needn't show every extreme that they name: `route_ids`: each row names 8 different experts; within each aligned block of 256 rows (the rows of one index of dp) no expert is named by more than 128 rows, and in some block some expert is named by exactly 128 rows.
All inputs are finite; a program needn't handle non-finite values.
Results may differ from a plain program's by a relative error of at most 0.0057.
Values may be sent and summed in bfloat16 or wider, within the bound.
A program may use at most 128 MiB of HBM per device.

v0:
```python
import jax
import jax.numpy as jnp
from jax import lax
from jax.sharding import PartitionSpec as P

EXP_DEV = 8


def route_slots(ids_rows, first_expert, expert_count, capacity):
    tok_rows, top_k = ids_rows.shape
    flat_ids = ids_rows.reshape(-1)
    local_ids = flat_ids - first_expert
    inside = (local_ids >= 0) & (local_ids < expert_count)
    safe_ids = jnp.where(inside, local_ids, 0)
    onehot = (safe_ids[:, None] == jnp.arange(expert_count, dtype=jnp.int32)[None, :]).astype(
        jnp.int32
    )
    onehot = onehot * inside.astype(jnp.int32)[:, None]
    running = jnp.cumsum(onehot, axis=0) - 1
    position = jnp.sum(onehot * running, axis=1)
    dump_slot = expert_count * capacity
    slot_index = jnp.where(inside, safe_ids * capacity + position, dump_slot)
    owner = jnp.arange(tok_rows * top_k, dtype=jnp.int32) // top_k
    slot_token = jnp.full((dump_slot + 1,), tok_rows, jnp.int32).at[slot_index].set(owner)
    return (slot_index, slot_token[:dump_slot])


def expert_rows(rows, gate_rows, up_rows, down_rows):
    dims = (((1,), (1,)), ((), ()))
    gate = lax.dot_general(rows, gate_rows, dims, preferred_element_type=jnp.float32)
    upper = lax.dot_general(rows, up_rows, dims, preferred_element_type=jnp.float32)
    act = (jax.nn.silu(gate) * upper).astype(jnp.bfloat16)
    return jnp.dot(act, down_rows, preferred_element_type=jnp.float32)


def body(tokens, route_ids, route_gates, gate_weight, up_weight, down_weight):
    gate_local = gate_weight[0]
    up_local = up_weight[0]
    down_local = down_weight[0]
    columns = lax.axis_size("expert")
    dp_count = lax.axis_size("dp")
    blocks = dp_count // EXP_DEV
    column = lax.axis_index("expert")
    rows_all = lax.all_gather(tokens, "expert", axis=1, tiled=True)
    tok_rows, top_k = route_ids.shape
    width = rows_all.shape[1]
    capacity = 2 * tok_rows * top_k // (EXP_DEV * columns)
    slot_index, slot_token = route_slots(route_ids, column * EXP_DEV, EXP_DEV, capacity)
    padded = jnp.concatenate([rows_all, jnp.zeros((1, width), jnp.bfloat16)], axis=0)
    buffer = padded[slot_token].reshape(EXP_DEV, capacity, width)
    copies = jnp.broadcast_to(buffer[:, None], (EXP_DEV, blocks, capacity, width))
    copies = copies.reshape(dp_count, capacity, width)
    received = lax.all_to_all(copies, "dp", split_axis=0, concat_axis=0, tiled=True)
    count = received.shape[1]
    flat = received.reshape(dp_count * count, width)
    part = expert_rows(flat, gate_local, up_local, down_local)
    part = part.reshape(dp_count, count, width)
    partials = lax.all_to_all(
        part.astype(jnp.bfloat16), "dp", split_axis=0, concat_axis=0, tiled=True
    ).astype(part.dtype)
    results = jnp.sum(partials.reshape(EXP_DEV, blocks, capacity, width), axis=1).astype(
        jnp.bfloat16
    )
    results = results.reshape(EXP_DEV * capacity, width)
    results_pad = jnp.concatenate([results, jnp.zeros((1, width), jnp.bfloat16)], axis=0)
    slot_rows = slot_index.reshape(tok_rows, top_k)
    mixed = jnp.zeros((tok_rows, width), jnp.float32)
    for route in range(top_k):
        picked = results_pad[slot_rows[:, route]]
        mixed = mixed + route_gates[:, route : route + 1] * picked.astype(jnp.float32)
    summed = lax.psum_scatter(mixed, "expert", scatter_dimension=1, tiled=True)
    return summed.astype(jnp.bfloat16)


def solution(mesh):
    placed = (
        P("dp", "expert"),
        P("dp", None),
        P("dp", None),
        P("expert", "dp", None),
        P("expert", "dp", None),
        P("expert", "dp", None),
    )
    return jax.shard_map(
        body, mesh=mesh, in_specs=placed, out_specs=P("dp", "expert"), check_vma=False
    )
```

profile of v0, /device:TPU:0, one launch (start us, length us, event | category | flops | bytes accessed | tf_op | source)
XLA Modules:
  0.0 597.8 jit_solution(11664268884255179119)
XLA Ops:
  6.5 0.0 all-gather.2.cloned.1.call-start
  6.5 0.7 all-gather.2.cloned.1.call-update
  7.3 0.8 copy.8
  8.1 0.1 sub.49
  8.2 0.1 sub.48
  8.3 0.1 sub.47
  8.5 2.3 reduce-window.6
  10.8 0.3 slice_reduce_fusion
  11.1 0.2 reduce-window.9
  11.3 0.1 add_bitcast_fusion
  11.4 8.0 %scatter_custom_fusion = s32[1025]{0:T(1024)S(1)} fusion(s32[2048]{0:T(1024)S(1)} %bitcast.49, s32[2048]{0:T(1024)S(1)} %add_select_fusion.1, s32[]{:T(128)} %constant.17.clone.1), kind=kCustom, calls=%fused_computation.69 | custom fusion | bytes 4104 | tf_op jit(solution)/shard_map/scatter | solution.py:24
  19.5 14.8 %all-gather.2.cloned.1.call-done = bf16[256,4096]{1,0:T(8,128)(2,1)} async-done(((bf16[256,1024]{1,0:T(8,128)(2,1)}), bf16[256,4096]{1,0:T(8,128)(2,1)}) %all-gather.2.cloned.1.call-update) | async-done | bytes 2097168 | tf_op jit(solution)/shard_map/all_gather | solution.py:44
  34.2 1.8 concatenate.6
  36.0 7.7 %gather_fusion = bf16[1024,4096]{1,0:T(8,128)(2,1)} fusion(bf16[257,4096]{1,0:T(8,128)(2,1)S(1)} %concatenate.6, s32[1024]{0:T(1024)S(1)} %fusion.25), kind=kCustom, calls=%fused_computation | custom fusion | bytes 16781312 | tf_op jit(solution)/shard_map/gather | solution.py:50
  43.8 0.0 slice-start
  43.8 189.7 %all_to_all.10 = bf16[8,128,4096]{2,1,0:T(8,128)(2,1)S(1)} all-to-all(bf16[8,128,4096]{2,1,0:T(8,128)(2,1)} %bitcast.44), channel_id=1, replica_groups=mesh['dp'=8,'expert'=4] {'dp'}, dimensions={0} | all-to-all | bytes 16777216 | tf_op jit(solution)/shard_map/all_to_all | solution.py:53
  233.5 0.0 slice-start.1
  233.5 0.0 slice-start.2
  233.5 11.3 %fusion.1 = f32[1024,768]{1,0:T(8,128)} fusion(bf16[1024,4096]{1,0:T(8,128)(2,1)S(1)} %bitcast.45, bf16[1,768,4096]{2,1,0:T(8,128)(2,1)} %param.10), kind=kOutput, calls=%fused_computation.12 | convolution fusion | flops 6442450944 | bytes 17825792 | tf_op jit(solution)/shard_map/dot_general | solution.py:31
  244.8 0.0 slice-done
  244.8 0.0 slice-done.1
  244.8 0.0 slice-start.3
  244.8 9.8 %multiply_convert_fusion = bf16[1024,768]{1,0:T(8,128)(2,1)} fusion(f32[1024,768]{1,0:T(8,128)} %fusion.1, bf16[1024,4096]{1,0:T(8,128)(2,1)S(1)} %bitcast.46, bf16[1,768,4096]{2,1,0:T(8,128)(2,1)S(1)} %bitcast.59), kind=kOutput, calls=%fused_computation.17 | convolution fusion | flops 6447169536 | bytes 19398656 | tf_op jit(solution)/shard_map/dot_general | solution.py:30
  254.5 0.0 slice-done.2
  254.5 0.0 slice-done.3
  254.5 10.3 %convolution_convert_fusion = bf16[8,128,4096]{2,1,0:T(8,128)(2,1)} fusion(bf16[8,128,768]{2,1,0:T(8,128)(2,1)} %bitcast.62, bf16[1,768,4096]{2,1,0:T(8,128)(2,1)S(1)} %bitcast.61), kind=kOutput, calls=%fused_computation.10 | convolution fusion | flops 6446645248 | bytes 16252928 | tf_op jit(solution)/shard_map/dot_general | solution.py:33
  264.8 0.0 copy-start
  264.8 5.2 all-to-all-start.1
  270.0 0.2 reduce-scatter.2.cloned.1.call-start
  270.2 0.1 reduce_sum.19
  270.3 0.6 fusion.7
  271.0 0.0 copy-done
  271.0 181.2 %all-to-all-done.1 = bf16[8,128,4096]{2,1,0:T(8,128)(2,1)} async-done(((bf16[8,128,4096]{2,1,0:T(8,128)(2,1)}), bf16[8,128,4096]{2,1,0:T(8,128)(2,1)}, u32[]{:S(2)}, u32[]{:S(2)}) %all-to-all-start.1) | async-done | bytes 8388640 | tf_op jit(solution)/shard_map/all_to_all | solution.py:58
  452.3 7.7 %concatenate.7 = bf16[1025,4096]{1,0:T(8,128)(2,1)} pad(bf16[1024,4096]{1,0:T(8,128)(2,1)} %bitcast.11, bf16[]{:T(256)} %constant.16.clone.1), padding=0_1x0_0 | pad | bytes 16785410 | tf_op jit(solution)/shard_map/concatenate | solution.py:65
  460.0 8.4 %gather_fusion.1 = bf16[256,4096]{1,0:T(8,128)(2,1)S(1)} fusion(bf16[1025,4096]{1,0:T(8,128)(2,1)} %concatenate.7, s32[1024]{0:T(1024)S(1)} %get-tuple-element.28), kind=kCustom, calls=%fused_computation.1 | custom fusion | bytes 4195328 | tf_op jit(solution)/shard_map/gather | solution.py:69
  468.4 9.7 %gather_fusion.2 = bf16[256,4096]{1,0:T(8,128)(2,1)} fusion(bf16[1025,4096]{1,0:T(8,128)(2,1)} %concatenate.7, s32[1024]{0:T(1024)S(1)} %get-tuple-element.27), kind=kCustom, calls=%fused_computation.2 | custom fusion | bytes 4195328 | tf_op jit(solution)/shard_map/gather | solution.py:69
  478.1 9.9 %gather_fusion.3 = bf16[256,4096]{1,0:T(8,128)(2,1)} fusion(bf16[1025,4096]{1,0:T(8,128)(2,1)} %concatenate.7, s32[1024]{0:T(1024)S(1)} %get-tuple-element.26), kind=kCustom, calls=%fused_computation.3 | custom fusion | bytes 4195328 | tf_op jit(solution)/shard_map/gather | solution.py:69
  487.9 9.7 %gather_fusion.4 = bf16[256,4096]{1,0:T(8,128)(2,1)} fusion(bf16[1025,4096]{1,0:T(8,128)(2,1)} %concatenate.7, s32[1024]{0:T(1024)S(1)} %get-tuple-element.25), kind=kCustom, calls=%fused_computation.4 | custom fusion | bytes 4195328 | tf_op jit(solution)/shard_map/gather | solution.py:69
  497.6 10.1 %gather_fusion.5 = bf16[256,4096]{1,0:T(8,128)(2,1)} fusion(bf16[1025,4096]{1,0:T(8,128)(2,1)} %concatenate.7, s32[1024]{0:T(1024)S(1)} %get-tuple-element.24), kind=kCustom, calls=%fused_computation.5 | custom fusion | bytes 4195328 | tf_op jit(solution)/shard_map/gather | solution.py:69
  507.7 9.7 %gather_fusion.6 = bf16[256,4096]{1,0:T(8,128)(2,1)} fusion(bf16[1025,4096]{1,0:T(8,128)(2,1)} %concatenate.7, s32[1024]{0:T(1024)S(1)} %get-tuple-element.23), kind=kCustom, calls=%fused_computation.6 | custom fusion | bytes 4195328 | tf_op jit(solution)/shard_map/gather | solution.py:69
  517.4 9.7 %gather_fusion.7 = bf16[256,4096]{1,0:T(8,128)(2,1)} fusion(bf16[1025,4096]{1,0:T(8,128)(2,1)} %concatenate.7, s32[1024]{0:T(1024)S(1)} %get-tuple-element.22), kind=kCustom, calls=%fused_computation.7 | custom fusion | bytes 4195328 | tf_op jit(solution)/shard_map/gather | solution.py:69
  527.1 9.9 %gather_fusion.8 = bf16[256,4096]{1,0:T(8,128)(2,1)} fusion(bf16[1025,4096]{1,0:T(8,128)(2,1)} %concatenate.7, s32[1024]{0:T(1024)S(1)} %get-tuple-element.21), kind=kCustom, calls=%fused_computation.8 | custom fusion | bytes 4195328 | tf_op jit(solution)/shard_map/gather | solution.py:69
  537.0 8.9 %multiply_add_fusion = f32[256,4096]{1,0:T(8,128)} fusion(bf16[256,4096]{1,0:T(8,128)(2,1)} %gather_fusion.8, bf16[256,4096]{1,0:T(8,128)(2,1)} %gather_fusion.7, bf16[256,4096]{1,0:T(8,128)(2,1)} %gather_fusion.6, bf16[256,4096]{1,0:T(8,128)(2,1)} %gather_fusion.5, bf16[256,4096]{1,0:T(8,128)(2,1)} %gather_fusion.4, bf16[256,4096]{1,0:T(8,128)(2,1)} %gather_fusion.3, ...), kind=kLoop, calls=%fused_computation.16 | loop fusion | flops 24117248 | bytes 20979712 | tf_op jit(solution)/shard_map/add | solution.py:70
  545.9 0.0 reduce-scatter.2.cloned.1.call-update
  545.9 42.8 %reduce-scatter.2.cloned.1.call-done = f32[256,1024]{1,0:T(8,128)} async-done(((f32[256,4096]{1,0:T(8,128)}), f32[256,1024]{1,0:T(8,128)}) %reduce-scatter.2.cloned.1.call-update) | async-done | bytes 1048592 | tf_op jit(solution)/shard_map/reduce_scatter | solution.py:71
  588.7 2.1 convert_element_type.63
  (18 shorter events, 0.2 us)
Async XLA Ops:
  6.5 27.7 %all-gather.2.cloned.1.call-start = ((), (), s32[]{:S(2)}) async-start(), calls=%async_computation.3 | async-start | bytes 2621440 | tf_op jit(solution)/shard_map/all_gather | solution.py:44
  43.8 201.0 %slice-start = ((s8[6291456]{0:T(1024)(128)(4,1)}), s8[4194304]{0:T(1024)(128)(4,1)S(1)}, s32[]{:S(2)}) async-start(s8[6291456]{0:T(1024)(128)(4,1)} %bitcast.58), calls=%async_computation.5 | async-start | bytes 8388608
  233.5 11.3 %slice-start.1 = ((s8[6291456]{0:T(1024)(128)(4,1)}), s8[2097152]{0:T(1024)(128)(4,1)S(1)}, s32[]{:S(2)}) async-start(s8[6291456]{0:T(1024)(128)(4,1)} %bitcast.58), calls=%async_computation.6 | async-start | bytes 4194304
  233.5 21.1 %slice-start.2 = ((s8[6291456]{0:T(1024)(128)(4,1)}), s8[4194304]{0:T(1024)(128)(4,1)S(1)}, s32[]{:S(2)}) async-start(s8[6291456]{0:T(1024)(128)(4,1)} %bitcast.60), calls=%async_computation.7 | async-start | bytes 8388608
  244.8 9.8 %slice-start.3 = ((s8[6291456]{0:T(1024)(128)(4,1)}), s8[2097152]{0:T(1024)(128)(4,1)S(1)}, s32[]{:S(2)}) async-start(s8[6291456]{0:T(1024)(128)(4,1)} %bitcast.60), calls=%async_computation.8 | async-start | bytes 4194304
  264.8 6.2 %copy-start = (f32[256,8]{0,1:T(8,128)S(1)}, f32[256,8]{0,1:T(8,128)}, u32[]{:S(2)}) copy-start(f32[256,8]{0,1:T(8,128)} %param.8) | copy-start | bytes 24580
  264.8 187.5 %all-to-all-start.1 = ((bf16[8,128,4096]{2,1,0:T(8,128)(2,1)}), bf16[8,128,4096]{2,1,0:T(8,128)(2,1)}, u32[]{:S(2)}, u32[]{:S(2)}) async-start(bf16[8,128,4096]{2,1,0:T(8,128)(2,1)} %convolution_convert_fusion), calls=%async_computation.1 | async-start | bytes 16777216 | tf_op jit(solution)/shard_map/all_to_all | solution.py:58
  270.0 318.7 %reduce-scatter.2.cloned.1.call-start = ((), (), s32[]{:S(2)}) async-start(), calls=%async_computation.4 | async-start | bytes 5242880 | tf_op jit(solution)/shard_map/reduce_scatter | solution.py:71
Sparse Core Ops, SparseCore 0:
  8.9 25.2 all-gather.1
  546.0 42.6 reduce-scatter.1
where the time goes:
time: 601 us; the launch traced here: 598 us
  waiting for transfers between devices  239 us (40%)
  blocking collectives  190 us (32%)
  local copies, waits for them, and re-layouts  104 us (17%)
  matrix products  31.3 us (5%)
  other arithmetic  14.3 us (2%)
  between operations  13.8 us (2%)
    all_to_all x1, blocking collectives, body(): lax.all_to_all(copies, 'dp', split_axis=0, concat_axis=0, tiled=True)  190 us
    all_to_all x1, waiting for transfers between devices, body(): lax.all_to_all(part.astype(jnp.bfloat16), 'dp', split_axis=0, concat_axis...  181 us
    gather x8, local copies, waits for them, and re-layouts, body(): picked = results_pad[slot_rows[:, route]]  77 us
    reduce_scatter x1, waiting for transfers between devices, body(): summed = lax.psum_scatter(mixed, 'expert', scatter_dimension=1, tiled=True)  42.8 us
    all_gather x1, waiting for transfers between devices, body(): rows_all = lax.all_gather(tokens, 'expert', axis=1, tiled=True)  14.8 us
  transfers between devices with their start and end apart: 3, of which 3 were waited for; matrix products, arithmetic and copies ran while one was open for 2% of the time, Pallas kernels for 0%

commit v1 on v0

--- a/solution.py
+++ b/solution.py
@@ -1,9 +1,298 @@
 import jax
 import jax.numpy as jnp
 from jax import lax
+from jax.experimental import pallas as pl
+from jax.experimental.pallas import tpu as pltpu
 from jax.sharding import PartitionSpec as P
 
 EXP_DEV = 8
+MESH = pl.DeviceIdType.MESH
+ORDER = (0, 1, 3, 2)
+NAMES = (
+    [(n, d) for n in ("z", "rz") for d in (1, 2, 3)]
+    + [(n, d) for n in ("x", "y", "fx", "fy", "rx2", "ry2") for d in range(4)]
+    + [(n, d, i) for n in ("p", "rx1", "ry1") for d in range(4) for i in range(2)]
+    + [("s", d, i) for d in range(4) for i in range(5)]
+    + [("w", m) for m in range(1, 8)]
+)
+SLOT = {name: i for i, name in enumerate(NAMES)}
+
+
+def layer_kernel(
+    tok, wt, g_hbm, u_hbm, w_hbm, out, a, gates, gw, uw, dw, sb, rx1, ry1, rx2, ry2, rz,
+    act, col, send, recv, local,
+):
+    dp = lax.axis_index("dp")
+    ex = lax.axis_index("expert")
+    z, x = dp // 2, dp % 2
+    y, k = ex // 2, ex % 2
+    tr, tc = tok.shape
+    half = tr // 2
+    hid = gw.shape[0]
+    x_dev = (z * 2 + (1 - x), ex)
+    y_dev = (dp, (1 - y) * 2 + k)
+    s_dev = (dp, y * 2 + (1 - k))
+
+    def z_dev(d):
+        return (((z + d) % 4) * 2 + x, ex)
+
+    def row(d, xx):
+        return pl.multiple_of((((z + d) % 4) * 2 + xx) * tr, tr)
+
+    def cols(yy, kk):
+        return pl.ds(pl.multiple_of((yy * 2 + kk) * tc, tc), tc)
+
+    def blk(d, xx, yy, kk, part=None):
+        if part is None:
+            return a.at[pl.ds(row(d, xx), tr), cols(yy, kk)]
+        start = pl.multiple_of(row(d, xx) + part * half, half)
+        return a.at[pl.ds(start, half), cols(yy, kk)]
+
+    def copy(name, src, dst, dev, there=None):
+        return pltpu.make_async_remote_copy(
+            src_ref=src,
+            dst_ref=dst,
+            send_sem=send.at[SLOT[name]],
+            recv_sem=recv.at[SLOT[there or name]],
+            device_id=dev,
+            device_id_type=MESH,
+        )
+
+    sent = {}
+
+    def go(name, src, dst, dev, there=None):
+        c = copy(name, src, dst, dev, there)
+        c.start()
+        sent[name] = c
+
+    def got(name, dst, dev):
+        copy(name, dst, dst, dev).wait_recv()
+
+    def drain(name):
+        sent.pop(name).wait_send()
+
+    barrier = pltpu.get_barrier_semaphore()
+    for m in range(1, 8):
+        pl.semaphore_signal(barrier, inc=1, device_id=((dp + m) % 8, ex), device_id_type=MESH)
+    for dev in (y_dev, s_dev):
+        pl.semaphore_signal(barrier, inc=1, device_id=dev, device_id_type=MESH)
+    pl.semaphore_wait(barrier, 9)
+
+    mine = blk(0, x, y, k)
+    go(("x", 0), tok, mine, x_dev)
+    go(("y", 0), tok, mine, y_dev)
+    for d in (1, 3, 2):
+        go(("z", d), tok, mine, z_dev(d), ("z", 4 - d))
+    go(("s", 0, 0), tok, mine, s_dev)
+    for m in range(1, 8):
+        go(("w", m), wt, gates.at[dp], ((dp + m) % 8, ex), ("w", 8 - m))
+    loads = [
+        pltpu.make_async_copy(src, dst, local.at[i])
+        for i, (src, dst) in enumerate(
+            ((tok, mine), (wt, gates.at[dp]), (g_hbm, gw), (u_hbm, uw), (w_hbm, dw))
+        )
+    ]
+    for load in loads:
+        load.start()
+
+    def pass_z(d):
+        b = blk(d, x, y, k)
+        got(("z", d), b, z_dev(d))
+        go(("x", d), b, b, x_dev)
+        go(("y", d), b, b, y_dev)
+        go(("s", d, 0), b, b, s_dev)
+
+    def pass_xy(d):
+        b = blk(d, 1 - x, y, k)
+        got(("x", d), b, x_dev)
+        h = blk(d, 1 - x, y, k, 0)
+        go(("fy", d), h, h, y_dev)
+        go(("s", d, 1), b, b, s_dev)
+        b = blk(d, x, 1 - y, k)
+        got(("y", d), b, y_dev)
+        h = blk(d, x, 1 - y, k, 1)
+        go(("fx", d), h, h, x_dev)
+        go(("s", d, 2), b, b, s_dev)
+
+    def pass_far(d):
+        h = blk(d, 1 - x, 1 - y, k, 0)
+        got(("fy", d), h, y_dev)
+        go(("s", d, 3), h, h, s_dev)
+        h = blk(d, 1 - x, 1 - y, k, 1)
+        got(("fx", d), h, x_dev)
+        go(("s", d, 4), h, h, s_dev)
+
+    def complete(d):
+        got(("s", d, 0), blk(d, x, y, 1 - k), s_dev)
+        got(("s", d, 1), blk(d, 1 - x, y, 1 - k), s_dev)
+        got(("s", d, 2), blk(d, x, 1 - y, 1 - k), s_dev)
+        got(("s", d, 3), blk(d, 1 - x, 1 - y, 1 - k, 0), s_dev)
+        got(("s", d, 4), blk(d, 1 - x, 1 - y, 1 - k, 1), s_dev)
+
+    dims = (((1,), (1,)), ((), ()))
+
+    def hidden(d):
+        rows = pl.ds(pl.multiple_of(((z + d) % 4) * 2 * tr, 2 * tr), 2 * tr)
+
+        @pl.loop(0, hid // 256)
+        def _(i):
+            hs = pl.ds(pl.multiple_of(i * 256, 256), 256)
+            g = lax.dot_general(a[rows, :], gw[hs, :], dims, preferred_element_type=jnp.float32)
+            u = lax.dot_general(a[rows, :], uw[hs, :], dims, preferred_element_type=jnp.float32)
+            act[:, hs] = ((g / (1.0 + jnp.exp(-g))) * u).astype(jnp.bfloat16)
+
+        for xx in range(2):
+            table = gates[((z + d) % 4) * 2 + xx]
+            pick = lax.broadcasted_iota(jnp.int32, table.shape, 0) == dp
+            line = jnp.sum(jnp.where(pick, table, 0.0), axis=0, keepdims=True)
+            col[xx * tr : (xx + 1) * tr, :] = jnp.broadcast_to(line, (128, tr)).T
+
+    def project(d):
+        rows = pl.ds(pl.multiple_of(((z + d) % 4) * 2 * tr, 2 * tr), 2 * tr)
+        for name in [("x", d), ("y", d), ("fx", d), ("fy", d)] + [("s", d, i) for i in range(5)]:
+            drain(name)
+
+        @pl.loop(0, a.shape[1] // 512)
+        def _(i):
+            cs = pl.ds(pl.multiple_of(i * 512, 512), 512)
+            r = jnp.dot(act[...], dw[:, cs], preferred_element_type=jnp.float32)
+            a[rows, cs] = (r * col[:, 0:1]).astype(jnp.bfloat16)
+
+    def add(start, count, cs, extra):
+        step = 64
+
+        @pl.loop(0, count // step)
+        def _(i):
+            o = pl.multiple_of(i * step, step)
+            rows = pl.ds(pl.multiple_of(start + o, step), step)
+            a[rows, cs] = (
+                a[rows, cs].astype(jnp.float32) + extra[pl.ds(o, step), :].astype(jnp.float32)
+            ).astype(jnp.bfloat16)
+
+    def reduce0(d):
+        rows = pl.ds(pl.multiple_of(((z + d) % 4) * 2 * tr, 2 * tr), 2 * tr)
+        for yy in range(2):
+            go(("p", d, yy), a.at[rows, cols(yy, 1 - k)], sb.at[d, yy], s_dev)
+
+    def reduce1(d):
+        start = pl.multiple_of(((z + d) % 4) * 2 * tr, 2 * tr)
+        for yy in range(2):
+            got(("p", d, yy), sb.at[d, yy], s_dev)
+            add(start, 2 * tr, cols(yy, k), sb.at[d, yy])
+        for i in range(2):
+            go(("ry1", d, i), blk(d, i, 1 - y, k, 0), ry1.at[d, i], y_dev)
+            go(("rx1", d, i), blk(d, 1 - x, i, k, 1), rx1.at[d, i], x_dev)
+
+    def reduce2(d):
+        for i in range(2):
+            got(("ry1", d, i), ry1.at[d, i], y_dev)
+            add(row(d, i), half, cols(y, k), ry1.at[d, i])
+        go(("rx2", d), blk(d, 1 - x, y, k, 0), rx2.at[d], x_dev)
+        for i in range(2):
+            got(("rx1", d, i), rx1.at[d, i], x_dev)
+            add(row(d, x) + half, half, cols(i, k), rx1.at[d, i])
+        go(("ry2", d), blk(d, x, 1 - y, k, 1), ry2.at[d], y_dev)
+
+    def reduce3(d):
+        got(("rx2", d), rx2.at[d], x_dev)
+        add(row(d, x), half, cols(y, k), rx2.at[d])
+        got(("ry2", d), ry2.at[d], y_dev)
+        add(row(d, x) + half, half, cols(y, k), ry2.at[d])
+        if d:
+            go(("rz", d), blk(d, x, y, k), rz.at[3 - d], z_dev(d), ("rz", 4 - d))
+
+    pass_xy(0)
+    for d in (1, 3, 2):
+        pass_z(d)
+    loads[0].wait()
+    pass_far(0)
+    loads[1].wait()
+    for m in range(1, 8):
+        got(("w", m), gates.at[(dp + m) % 8], ((dp + m) % 8, ex))
+    for load in loads[2:]:
+        load.wait()
+
+    for i, d in enumerate(ORDER):
+        complete(d)
+        hidden(d)
+        if i < 3:
+            pass_xy(ORDER[i + 1])
+        project(d)
+        reduce0(d)
+        if i < 3:
+            pass_far(ORDER[i + 1])
+        if i >= 1:
+            reduce1(ORDER[i - 1])
+        if i >= 2:
+            reduce2(ORDER[i - 2])
+        if i >= 3:
+            reduce3(ORDER[i - 3])
+    reduce1(ORDER[3])
+    reduce2(ORDER[2])
+    reduce3(ORDER[1])
+    reduce2(ORDER[3])
+    reduce3(ORDER[2])
+    reduce3(ORDER[3])
+    for d in (1, 2, 3):
+        got(("rz", d), rz.at[d - 1], z_dev(d))
+
+    @pl.loop(0, tr // 64)
+    def _(i):
+        o = pl.multiple_of(i * 64, 64)
+        total = a[pl.ds(pl.multiple_of(row(0, x) + o, 64), 64), cols(y, k)].astype(jnp.float32)
+        for d in range(3):
+            total = total + rz[d, pl.ds(o, 64), :].astype(jnp.float32)
+        out[pl.ds(o, 64), :] = total.astype(jnp.bfloat16)
+
+    for name in list(sent):
+        drain(name)
+
+
+def fused_body(tokens, route_ids, route_gates, gate_weight, up_weight, down_weight):
+    tr, tc = tokens.shape
+    width = gate_weight.shape[2]
+    hid = gate_weight.shape[1]
+    experts = lax.axis_index("expert") * EXP_DEV + jnp.arange(EXP_DEV, dtype=jnp.int32)
+    hit = route_ids[None, :, :] == experts[:, None, None]
+    wt = jnp.sum(jnp.where(hit, route_gates[None, :, :], 0.0), axis=2)
+    half = tr // 2
+    bf = jnp.bfloat16
+    return pl.pallas_call(
+        layer_kernel,
+        out_shape=jax.ShapeDtypeStruct((tr, tc), bf),
+        in_specs=[
+            pl.BlockSpec(memory_space=pl.ANY),
+            pl.BlockSpec(memory_space=pltpu.VMEM),
+            pl.BlockSpec(memory_space=pl.ANY),
+            pl.BlockSpec(memory_space=pl.ANY),
+            pl.BlockSpec(memory_space=pl.ANY),
+        ],
+        out_specs=pl.BlockSpec(memory_space=pltpu.VMEM),
+        scratch_shapes=[
+            pltpu.VMEM((8 * tr, width), bf),
+            pltpu.VMEM((8, EXP_DEV, tr), jnp.float32),
+            pltpu.VMEM((hid, width), bf),
+            pltpu.VMEM((hid, width), bf),
+            pltpu.VMEM((hid, width), bf),
+            pltpu.VMEM((4, 2, 2 * tr, tc), bf),
+            pltpu.VMEM((4, 2, half, tc), bf),
+            pltpu.VMEM((4, 2, half, tc), bf),
+            pltpu.VMEM((4, half, tc), bf),
+            pltpu.VMEM((4, half, tc), bf),
+            pltpu.VMEM((3, tr, tc), bf),
+            pltpu.VMEM((2 * tr, hid), bf),
+            pltpu.VMEM((2 * tr, 128), jnp.float32),
+            pltpu.SemaphoreType.DMA((len(NAMES),)),
+            pltpu.SemaphoreType.DMA((len(NAMES),)),
+            pltpu.SemaphoreType.DMA((5,)),
+        ],
+        compiler_params=pltpu.CompilerParams(
+            collective_id=0, has_side_effects=True, vmem_limit_bytes=60 * 1024 * 1024
+        ),
+        cost_estimate=pl.CostEstimate(
+            flops=6 * 8 * tr * width * hid, bytes_accessed=6 * width * hid, transcendentals=0
+        ),
+    )(tokens, wt, gate_weight[0], up_weight[0], down_weight[0])
 
 
 def route_slots(ids_rows, first_expert, expert_count, capacity):
@@ -81,6 +370,7 @@
         P("expert", "dp", None),
         P("expert", "dp", None),
     )
+    small = mesh.shape["dp"] == 8 and mesh.shape["expert"] == 4
     return jax.shard_map(
-        body, mesh=mesh, in_specs=placed, out_specs=P("dp", "expert"), check_vma=False
+        fused_body if small else body, mesh=mesh, in_specs=placed, out_specs=P("dp", "expert"), check_vma=False
     )

time: 601 us -> 201 us (0.33)
  waiting for transfers between devices: 239 us -> 0 us
  Pallas kernels: 0 us -> 197 us
  blocking collectives: 190 us -> 0 us
  local copies, waits for them, and re-layouts: 104 us -> 1.87 us
  matrix products: 31.3 us -> 0 us
  between operations: 13.8 us -> 0.01 us
  other arithmetic: 14.3 us -> 1.41 us
    pallas_call x0 -> x1, Pallas kernels: none -> 197 us  [fused_body(): pl.pallas_call(layer_kernel, out_shape=jax.ShapeDtypeStruct((tr, tc), bf)...]
    all_to_all x1 -> x0, blocking collectives: 190 us -> none  [body(): lax.all_to_all(copies, 'dp', split_axis=0, concat_axis=0, tiled=True)]
    all_to_all x1 -> x0, waiting for transfers between devices: 181 us -> none  [body(): lax.all_to_all(part.astype(jnp.bfloat16), 'dp', split_axis=0, concat_axis...]
    gather x9 -> x0, local copies, waits for them, and re-layouts: 84.7 us -> none  [the longest x8 77 us: body(): picked = results_pad[slot_rows[:, route]]]
    reduce_scatter x1 -> x0, waiting for transfers between devices: 42.8 us -> none  [body(): summed = lax.psum_scatter(mixed, 'expert', scatter_dimension=1, tiled=True)]
    dot_general x3 -> x0, matrix products: 31.3 us -> none  [the longest x1 11.3 us: expert_rows(): lax.dot_general(rows, up_rows, dims, preferred_element_type=jnp.float32)]
    all_gather x1 -> x0, waiting for transfers between devices: 14.8 us -> none  [body(): rows_all = lax.all_gather(tokens, 'expert', axis=1, tiled=True)]
    concatenate x2 -> x0, local copies, waits for them, and re-layouts: 9.51 us -> none  [the longest x1 7.73 us: body(): jnp.concatenate([results, jnp.zeros((1, width), jnp.bfloat16)], axis=0)]
  transfers between devices with their start and end apart: 3 -> 0, of which waited for: 3 -> 0; matrix products, arithmetic and copies ran while one was open for 2% -> 0% of each run, Pallas kernels for 0% -> 0%
where the time goes in v1:
time: 201 us; the launch traced here: 200 us
  Pallas kernels  197 us (98%)
    pallas_call x1, Pallas kernels, fused_body(): pl.pallas_call(layer_kernel, out_shape=jax.ShapeDtypeStruct((tr, tc), bf)...  197 us

profile of v1, /device:TPU:0, one launch (start us, length us, event | category | flops | bytes accessed | tf_op | source)
XLA Modules:
  0.0 200.4 jit_solution(9481678693587783499)
XLA Ops:
  0.0 1.4 select_reduce_fusion.wt
  1.4 197.1 %shard_map.64 = bf16[256,1024]{1,0:T(8,128)(2,1)} custom-call(bf16[256,1024]{1,0:T(8,128)(2,1)} %tok.1, f32[8,256]{1,0:T(8,128)} %select_reduce_fusion.wt, bf16[768,4096]{1,0:T(8,128)(2,1)} %bitcast.3, bf16[768,4096]{1,0:T(8,128)(2,1)} %bitcast.4, bf16[768,4096]{1,0:T(8,128)(2,1)} %bitcast.5), custom_call_target="tpu_custom_call" | custom-call | flops 38654705664 | bytes 18874368 | tf_op jit(solution)/shard_map/pallas_call | solution.py:260
  198.5 1.9 copy.10
  (1 shorter events, 0.0 us)

commit v2 on v1

--- a/solution.py
+++ b/solution.py
@@ -7,7 +7,7 @@
 
 EXP_DEV = 8
 MESH = pl.DeviceIdType.MESH
-ORDER = (0, 1, 3, 2)
+ORDER = (0, 3, 2, 1)
 NAMES = (
     [(n, d) for n in ("z", "rz") for d in (1, 2, 3)]
     + [(n, d) for n in ("x", "y", "fx", "fy", "rx2", "ry2") for d in range(4)]
@@ -81,7 +81,7 @@
     mine = blk(0, x, y, k)
     go(("x", 0), tok, mine, x_dev)
     go(("y", 0), tok, mine, y_dev)
-    for d in (1, 3, 2):
+    for d in (3, 2, 1):
         go(("z", d), tok, mine, z_dev(d), ("z", 4 - d))
     go(("s", 0, 0), tok, mine, s_dev)
     for m in range(1, 8):
@@ -202,7 +202,7 @@
             go(("rz", d), blk(d, x, y, k), rz.at[3 - d], z_dev(d), ("rz", 4 - d))
 
     pass_xy(0)
-    for d in (1, 3, 2):
+    for d in (3, 2, 1):
         pass_z(d)
     loads[0].wait()
     pass_far(0)

time: 201 us -> 213 us (1.060)
  Pallas kernels: 197 us -> 209 us
    pallas_call x1, Pallas kernels: 197 us -> 209 us  [fused_body(): pl.pallas_call(layer_kernel, out_shape=jax.ShapeDtypeStruct((tr, tc), bf)...]
where the time goes in v2:
time: 213 us
  Pallas kernels  209 us (98%)
    pallas_call x1, Pallas kernels, fused_body(): pl.pallas_call(layer_kernel, out_shape=jax.ShapeDtypeStruct((tr, tc), bf)...  209 us

profile of v2, /device:TPU:0, one launch (start us, length us, event | category | flops | bytes accessed | tf_op | source)
XLA Modules:
  0.0 212.6 jit_solution(12539596305669625308)
XLA Ops:
  0.0 1.4 select_reduce_fusion.wt
  1.4 209.3 %shard_map.64 = bf16[256,1024]{1,0:T(8,128)(2,1)} custom-call(bf16[256,1024]{1,0:T(8,128)(2,1)} %tok.1, f32[8,256]{1,0:T(8,128)} %select_reduce_fusion.wt, bf16[768,4096]{1,0:T(8,128)(2,1)} %bitcast.3, bf16[768,4096]{1,0:T(8,128)(2,1)} %bitcast.4, bf16[768,4096]{1,0:T(8,128)(2,1)} %bitcast.5), custom_call_target="tpu_custom_call" | custom-call | flops 38654705664 | bytes 18874368 | tf_op jit(solution)/shard_map/pallas_call | solution.py:260
  210.8 1.9 copy.10
  (1 shorter events, 0.0 us)

commit v3 on v2

--- a/solution.py
+++ b/solution.py
@@ -7,7 +7,7 @@
 
 EXP_DEV = 8
 MESH = pl.DeviceIdType.MESH
-ORDER = (0, 3, 2, 1)
+ORDER = (0, 1, 2, 3)
 NAMES = (
     [(n, d) for n in ("z", "rz") for d in (1, 2, 3)]
     + [(n, d) for n in ("x", "y", "fx", "fy", "rx2", "ry2") for d in range(4)]
@@ -26,6 +26,8 @@
     ex = lax.axis_index("expert")
     z, x = dp // 2, dp % 2
     y, k = ex // 2, ex % 2
+    turn = 1 - 2 * (z // 2)
+    back = 3 - 2 * (((z + 1) // 2) % 2)
     tr, tc = tok.shape
     half = tr // 2
     hid = gw.shape[0]
@@ -34,10 +36,13 @@
     s_dev = (dp, y * 2 + (1 - k))
 
     def z_dev(d):
-        return (((z + d) % 4) * 2 + x, ex)
+        return (((z + 4 + turn * d) % 4) * 2 + x, ex)
+
+    def seen(d):
+        return 2 if d == 2 else back
 
     def row(d, xx):
-        return pl.multiple_of((((z + d) % 4) * 2 + xx) * tr, tr)
+        return pl.multiple_of((((z + 4 + turn * d) % 4) * 2 + xx) * tr, tr)
 
     def cols(yy, kk):
         return pl.ds(pl.multiple_of((yy * 2 + kk) * tc, tc), tc)
@@ -53,7 +58,7 @@
             src_ref=src,
             dst_ref=dst,
             send_sem=send.at[SLOT[name]],
-            recv_sem=recv.at[SLOT[there or name]],
+            recv_sem=recv.at[SLOT[name] if there is None else there],
             device_id=dev,
             device_id_type=MESH,
         )
@@ -81,11 +86,11 @@
     mine = blk(0, x, y, k)
     go(("x", 0), tok, mine, x_dev)
     go(("y", 0), tok, mine, y_dev)
-    for d in (3, 2, 1):
-        go(("z", d), tok, mine, z_dev(d), ("z", 4 - d))
+    for d in (1, 2, 3):
+        go(("z", d), tok, mine, z_dev(d), SLOT["z", 1] + seen(d) - 1)
     go(("s", 0, 0), tok, mine, s_dev)
     for m in range(1, 8):
-        go(("w", m), wt, gates.at[dp], ((dp + m) % 8, ex), ("w", 8 - m))
+        go(("w", m), wt, gates.at[dp], ((dp + m) % 8, ex), SLOT["w", 8 - m])
     loads = [
         pltpu.make_async_copy(src, dst, local.at[i])
         for i, (src, dst) in enumerate(
@@ -132,7 +137,7 @@
     dims = (((1,), (1,)), ((), ()))
 
     def hidden(d):
-        rows = pl.ds(pl.multiple_of(((z + d) % 4) * 2 * tr, 2 * tr), 2 * tr)
+        rows = pl.ds(pl.multiple_of(((z + 4 + turn * d) % 4) * 2 * tr, 2 * tr), 2 * tr)
 
         @pl.loop(0, hid // 256)
         def _(i):
@@ -142,13 +147,13 @@
             act[:, hs] = ((g / (1.0 + jnp.exp(-g))) * u).astype(jnp.bfloat16)
 
         for xx in range(2):
-            table = gates[((z + d) % 4) * 2 + xx]
+            table = gates[((z + 4 + turn * d) % 4) * 2 + xx]
             pick = lax.broadcasted_iota(jnp.int32, table.shape, 0) == dp
             line = jnp.sum(jnp.where(pick, table, 0.0), axis=0, keepdims=True)
             col[xx * tr : (xx + 1) * tr, :] = jnp.broadcast_to(line, (128, tr)).T
 
     def project(d):
-        rows = pl.ds(pl.multiple_of(((z + d) % 4) * 2 * tr, 2 * tr), 2 * tr)
+        rows = pl.ds(pl.multiple_of(((z + 4 + turn * d) % 4) * 2 * tr, 2 * tr), 2 * tr)
         for name in [("x", d), ("y", d), ("fx", d), ("fy", d)] + [("s", d, i) for i in range(5)]:
             drain(name)
 
@@ -170,12 +175,12 @@
             ).astype(jnp.bfloat16)
 
     def reduce0(d):
-        rows = pl.ds(pl.multiple_of(((z + d) % 4) * 2 * tr, 2 * tr), 2 * tr)
+        rows = pl.ds(pl.multiple_of(((z + 4 + turn * d) % 4) * 2 * tr, 2 * tr), 2 * tr)
         for yy in range(2):
             go(("p", d, yy), a.at[rows, cols(yy, 1 - k)], sb.at[d, yy], s_dev)
 
     def reduce1(d):
-        start = pl.multiple_of(((z + d) % 4) * 2 * tr, 2 * tr)
+        start = pl.multiple_of(((z + 4 + turn * d) % 4) * 2 * tr, 2 * tr)
         for yy in range(2):
             got(("p", d, yy), sb.at[d, yy], s_dev)
             add(start, 2 * tr, cols(yy, k), sb.at[d, yy])
@@ -199,11 +204,10 @@
         got(("ry2", d), ry2.at[d], y_dev)
         add(row(d, x) + half, half, cols(y, k), ry2.at[d])
         if d:
-            go(("rz", d), blk(d, x, y, k), rz.at[3 - d], z_dev(d), ("rz", 4 - d))
+            go(("rz", d), blk(d, x, y, k), rz.at[seen(d) - 1], z_dev(d), SLOT["rz", 1] + seen(d) - 1)
 
     pass_xy(0)
-    for d in (3, 2, 1):
-        pass_z(d)
+    pass_z(1)
     loads[0].wait()
     pass_far(0)
     loads[1].wait()
@@ -215,10 +219,14 @@
     for i, d in enumerate(ORDER):
         complete(d)
         hidden(d)
+        if i == 0:
+            pass_z(2)
         if i < 3:
             pass_xy(ORDER[i + 1])
         project(d)
         reduce0(d)
+        if i == 0:
+            pass_z(3)
         if i < 3:
             pass_far(ORDER[i + 1])
         if i >= 1:

time: 213 us -> 215 us (level)
  Pallas kernels: 209 us -> 212 us
    pallas_call x1, Pallas kernels: 209 us -> 212 us  [fused_body(): pl.pallas_call(layer_kernel, out_shape=jax.ShapeDtypeStruct((tr, tc), bf)...]
where the time goes in v3:
time: 215 us
  Pallas kernels  212 us (99%)
    pallas_call x1, Pallas kernels, fused_body(): pl.pallas_call(layer_kernel, out_shape=jax.ShapeDtypeStruct((tr, tc), bf)...  212 us

profile of v3, /device:TPU:0, one launch (start us, length us, event | category | flops | bytes accessed | tf_op | source)
XLA Modules:
  0.0 214.8 jit_solution(2084844777555768708)
XLA Ops:
  0.0 1.4 select_reduce_fusion.wt
  1.4 211.6 %shard_map.64 = bf16[256,1024]{1,0:T(8,128)(2,1)} custom-call(bf16[256,1024]{1,0:T(8,128)(2,1)} %tok.1, f32[8,256]{1,0:T(8,128)} %select_reduce_fusion.wt, bf16[768,4096]{1,0:T(8,128)(2,1)} %bitcast.3, bf16[768,4096]{1,0:T(8,128)(2,1)} %bitcast.4, bf16[768,4096]{1,0:T(8,128)(2,1)} %bitcast.5), custom_call_target="tpu_custom_call" | custom-call | flops 38654705664 | bytes 18874368 | tf_op jit(solution)/shard_map/pallas_call | solution.py:268
  213.0 1.9 copy.10
  (1 shorter events, 0.0 us)
